TPU v7x, 768 devices: a whole 4x8x12 slice. The times are simulated.
768 devices in a mesh: node: 64 (over z_hi, y, x), chip: 6 (over z_lo), pair: 2 (over core).
Axes of the slice: x: 4, y: 8, z: 12 (z_hi: 2, z_lo: 6; z = z_hi * 6 + z_lo), core: 2. Of those that a mesh axis runs over, the one named last changes fastest.
Arguments:
- hidden: bfloat16 [98304, 6912], P(('node', 'chip', 'pair')), may hold values from -6 to 6
- cotangent: bfloat16 [98304, 2560], P('node'), may hold values from -0.4375 to 0.4375
Outputs:
- grad_weight: float32 [2560, 6912], P('node', ('chip', 'pair'))
All inputs are finite; a program needn't handle non-finite values.
Results may differ from a plain program's by a relative error of at most 0.0003.
Values may be sent and summed in bfloat16 or wider, within the bound.
No kernel may reach another device: no remote copies, remote signals or barrier semaphores. Data moves between devices by JAX's collectives and lax.ppermute only.
A program may use at most 64 MiB of HBM per device.

v0:
```python
import jax
import jax.numpy as jnp
from jax import lax
from jax.sharding import PartitionSpec as P


def shards(hidden, cotangent):
    moved = lax.all_to_all(hidden, ("chip", "pair"), split_axis=1, concat_axis=0, tiled=True)
    return lax.psum_scatter(
        lax.dot_general(
            cotangent, moved, (((0,), (0,)), ((), ())), preferred_element_type=jnp.float32
        ),
        "node",
        scatter_dimension=0,
        tiled=True,
    )


def solution(mesh):
    in_specs = (P(("node", "chip", "pair"), None), P("node", None))
    out_specs = P("node", ("chip", "pair"))
    return jax.shard_map(shards, mesh=mesh, in_specs=in_specs, out_specs=out_specs, check_vma=False)
```

profile of v0, /device:TPU:126, one launch (start us, length us, event | category | flops | bytes accessed | tf_op | source)
XLA Modules:
  0.0 696.4 jit_solution(5561742957398834617)
XLA Ops:
  6.5 0.0 reduce-scatter.5.cloned.1.call-start
  6.5 2.7 copy.5
  9.3 71.1 %all_to_all.19 = bf16[128,12,576]{0,2,1:T(8,128)(2,1)S(1)} all-to-all(bf16[128,12,576]{0,2,1:T(8,128)(2,1)S(1)} %bitcast.7), channel_id=1, replica_groups=mesh['node'=64,'chip'=6,'pair'=2] {'chip','pair'}, dimensions={1} | all-to-all | bytes 3538944 | tf_op jit(solution)/shard_map/all_to_all | solution.py:8
  80.4 2.3 copy.6
  82.7 11.0 %fusion = f32[2560,576]{1,0:T(8,128)} fusion(bf16[1536,2560]{1,0:T(8,128)(2,1)} %param.3, bf16[1536,576]{1,0:T(8,128)(2,1)} %bitcast.8), kind=kOutput, calls=%fused_computation | convolution fusion | flops 4529848320 | bytes 15532032 | tf_op jit(solution)/shard_map/dot_general | solution.py:10
  93.7 0.0 reduce-scatter.5.cloned.1.call-update
  93.7 595.8 %reduce-scatter.5.cloned.1.call-done = f32[40,576]{1,0:T(8,128)} async-done(((f32[2560,576]{1,0:T(8,128)}), f32[40,576]{1,0:T(8,128)}) %reduce-scatter.5.cloned.1.call-update) | async-done | bytes 92176
Async XLA Ops:
  6.5 683.0 %reduce-scatter.5.cloned.1.call-start = ((), (), s32[]{:S(2)}) async-start(), calls=%async_computation.2 | async-start | bytes 6656000
Sparse Core Ops, SparseCore 0:
  93.8 595.6 reduce-scatter.4
where the time goes:
time: 697 us; the launch traced here: 696 us
  waiting for transfers between devices  596 us (86%)
  blocking collectives  71.1 us (10%)
  between operations  13.4 us (2%)
  matrix products  11 us (2%)
    unnamed x2, waiting for transfers between devices  596 us
    all_to_all x1, blocking collectives, shards(): lax.all_to_all(hidden, ('chip', 'pair'), split_axis=1, concat_axis=0, til...  71.1 us
  transfers between devices with their start and end apart: 1, of which 1 were waited for; matrix products, arithmetic and copies ran while one was open for 0% of the time, Pallas kernels for 0%

commit v1 on v0

v1 whole, which is shorter than its diff:
```python
import jax
import jax.numpy as jnp
from jax import lax
from jax.sharding import Mesh, PartitionSpec as P

SIZES = {"zh": 2, "yh": 4, "yl": 2, "x": 4, "chip": 6, "pair": 2}
LIMIT = 60000.0


def decoded(code):
    return jnp.exp2(code)


def code_for(bound):
    e = jnp.floor(jnp.log2(LIMIT) - jnp.log2(jnp.maximum(bound, 1e-30)) - 0.01)
    return jnp.clip(e, -100.0, 100.0)


def shards(hidden, cotangent):
    t, ff = hidden.shape
    tokens, d = cotangent.shape
    groups = tokens // t
    w = ff // groups
    wide = -(-(w + 1) // 128) * 128
    near, far = SIZES["yl"] * SIZES["x"], SIZES["zh"] * SIZES["yh"]
    r = d // (near * far)

    part = lax.all_to_all(
        hidden.T.reshape(groups, w, t), ("chip", "pair"), split_axis=0, concat_axis=0, tiled=True
    )
    cot = cotangent.reshape(tokens, far, near, r).transpose(2, 1, 3, 0).reshape(d, tokens)
    top = jnp.max(jnp.abs(cotangent)).astype(jnp.float32)

    code = code_for(top * jnp.max(jnp.abs(part)).astype(jnp.float32) * tokens)
    part = part.transpose(1, 0, 2).reshape(w, tokens)
    part = jnp.pad(part, ((0, wide - w), (0, 0)))
    dims = (((1,), (1,)), ((), ()))
    lane = jnp.arange(wide) < w

    terms = lax.dot_general(cot, part, dims, preferred_element_type=jnp.float32)
    terms = jnp.where(lane, terms * decoded(code), code).astype(jnp.float16)
    got = lax.all_to_all(
        terms.reshape(near, d // near, wide), ("yl", "x"), split_axis=0, concat_axis=0, tiled=True
    )
    me = lax.axis_index(("yl", "x"))
    own = lax.dynamic_slice_in_dim(cot, me * (d // near), d // near, 0)
    own = lax.dot_general(own, part, dims, preferred_element_type=jnp.float32)
    back = decoded(-got[:, 0, w].astype(jnp.float32))
    others = (jnp.arange(near) != me)
    weight = jnp.where(others, back, 0.0)[:, None, None]
    row = (got.astype(jnp.float32) * weight).sum(0) + own

    code = code_for(LIMIT * back.sum())
    sent = jnp.where(lane, row * decoded(code), code).astype(jnp.float16)
    got = lax.all_to_all(
        sent.reshape(far, r, wide), ("zh", "yh"), split_axis=0, concat_axis=0, tiled=True
    )
    me = lax.axis_index(("zh", "yh"))
    own = lax.dynamic_slice_in_dim(row, me * r, r, 0)
    back = decoded(-got[:, 0, w].astype(jnp.float32))
    weight = jnp.where(jnp.arange(far) != me, back, 0.0)[:, None, None]
    return ((got.astype(jnp.float32) * weight).sum(0) + own)[:, :w]


def solution(mesh):
    fine = Mesh(mesh.devices.reshape(tuple(SIZES.values())), tuple(SIZES))
    node = ("zh", "yh", "yl", "x")
    in_specs = (P(node + ("chip", "pair"), None), P(node, None))
    out_specs = P(node, ("chip", "pair"))
    return jax.shard_map(shards, mesh=fine, in_specs=in_specs, out_specs=out_specs, check_vma=False)
```

time: 697 us -> 179 us (0.26)
  the two profiles are of different devices: /device:TPU:126 before, /device:TPU:10 now
where the time goes in v1:
time: 179 us; the launch traced here: 178 us
  waiting for transfers between devices  94.9 us (53%)
  starting transfers between devices  32.8 us (18%)
  local copies, waits for them, and re-layouts  28.7 us (16%)
  matrix products  11.8 us (7%)
  other arithmetic  8.17 us (5%)
  between operations  2.15 us (1%)
    all_to_all x1, waiting for transfers between devices, shards(): lax.all_to_all(hidden.T.reshape(groups, w, t), ('chip', 'pair'), split_ax...  39.3 us
    all_to_all x1, waiting for transfers between devices, shards(): lax.all_to_all(terms.reshape(near, d // near, wide), ('yl', 'x'), split_a...  37.3 us
    all_to_all x1, waiting for transfers between devices, shards(): lax.all_to_all(sent.reshape(far, r, wide), ('zh', 'yh'), split_axis=0, co...  18.3 us
    unnamed x4, local copies, waits for them, and re-layouts  15.3 us
    all_to_all x1, starting transfers between devices, shards(): lax.all_to_all(sent.reshape(far, r, wide), ('zh', 'yh'), split_axis=0, co...  14.9 us
    all_to_all x1, starting transfers between devices, shards(): lax.all_to_all(hidden.T.reshape(groups, w, t), ('chip', 'pair'), split_ax...  12.1 us
    dot_general x1, matrix products, shards(): terms = lax.dot_general(cot, part, dims, preferred_element_type=jnp.float32)  8.84 us
    transpose x1, local copies, waits for them, and re-layouts, shards(): cotangent.reshape(tokens, far, near, r).transpose(2, 1, 3, 0)  7.1 us
  transfers between devices with their start and end apart: 3, of which 3 were waited for; matrix products, arithmetic and copies ran while one was open for 13% of the time, Pallas kernels for 0%

profile of v1, /device:TPU:10, one launch (start us, length us, event | category | flops | bytes accessed | tf_op | source)
XLA Modules:
  0.0 178.4 jit_solution(11331679712618160380)
XLA Ops:
  0.0 3.8 %copy.10 = bf16[128,6912]{0,1:T(8,128)(2,1)} copy(bf16[128,6912]{1,0:T(8,128)(2,1)} %param.2) | data formatting | bytes 3538944 | tf_op args[0]
  3.8 12.1 %all-to-all-start = ((bf16[12,576,128]{2,1,0:T(8,128)(2,1)}), bf16[12,576,128]{2,1,0:T(8,128)(2,1)S(1)}, u32[]{:S(2)}, u32[]{:S(2)}) async-start(bf16[12,576,128]{2,1,0:T(8,128)(2,1)} %bitcast.1), calls=%async_computation | async-start | bytes 3538944 | tf_op jit(solution)/shard_map/all_to_all | solution.py:28
  16.0 10.7 %copy.12 = bf16[1536,2560]{0,1:T(8,128)(2,1)} copy(bf16[1536,2560]{1,0:T(8,128)(2,1)} %param.3) | data formatting | bytes 15728640 | tf_op args[1]
  26.6 7.1 %copy.13 = bf16[8,8,40,1536]{3,2,1,0:T(8,128)(2,1)} copy(bf16[8,8,40,1536]{3,2,0,1:T(8,128)(2,1)} %bitcast.14) | data formatting | bytes 15728640 | tf_op jit(solution)/shard_map/transpose | solution.py:31
  33.7 4.8 %abs_reduce_fusion = bf16[]{:T(256)} fusion(bf16[1536,2560]{1,0:T(8,128)(2,1)} %param.3), kind=kLoop, calls=%fused_computation | loop fusion | flops 7864319 | bytes 7864322 | tf_op jit(solution)/shard_map/reduce_max | solution.py:32
  38.6 39.3 %all-to-all-done = bf16[12,576,128]{2,1,0:T(8,128)(2,1)S(1)} async-done(((bf16[12,576,128]{2,1,0:T(8,128)(2,1)}), bf16[12,576,128]{2,1,0:T(8,128)(2,1)S(1)}, u32[]{:S(2)}, u32[]{:S(2)}) %all-to-all-start) | async-done | bytes 1769504 | tf_op jit(solution)/shard_map/all_to_all | solution.py:28
  77.9 0.9 abs_reduce_fusion.1
  80.1 2.3 %copy.11 = bf16[576,12,128]{0,2,1:T(8,128)(2,1)} copy(bf16[576,12,128]{2,0,1:T(8,128)(2,1)S(1)} %bitcast.15) | data formatting | bytes 3538944 | tf_op jit(solution)/shard_map/transpose | solution.py:35
  82.4 8.8 %fusion = f16[2560,640]{0,1:T(8,128)(2,1)S(1)} fusion(bf16[2560,1536]{1,0:T(8,128)(2,1)} %bitcast.17, f32[]{:T(128)S(6)} %min.7, f32[]{:T(128)S(6)} %exp2.31, pred[640]{0:T(1024)(128)(4,1)S(1)} %iota_compare_fusion, bf16[576,1536]{0,1:T(8,128)(2,1)} %bitcast.19), kind=kOutput, calls=%fused_computation.3 | convolution fusion | flops 5038080000 | bytes 12911240 | tf_op jit(solution)/shard_map/dot_general | solution.py:40
  91.3 4.0 %copy.14 = f16[2560,640]{1,0:T(8,128)(2,1)} copy(f16[2560,640]{0,1:T(8,128)(2,1)S(1)} %fusion) | data formatting | bytes 6553600 | tf_op jit(solution)/shard_map/convert_element_type | solution.py:41
  95.2 5.7 %all-to-all-start.1 = ((f16[8,320,640]{2,1,0:T(8,128)(2,1)}), f16[8,320,640]{2,1,0:T(8,128)(2,1)S(1)}, u32[]{:S(2)}, u32[]{:S(2)}) async-start(f16[8,320,640]{2,1,0:T(8,128)(2,1)} %bitcast.16), calls=%async_computation.1 | async-start | bytes 6553600 | tf_op jit(solution)/shard_map/all_to_all | solution.py:42
  101.0 37.3 %all-to-all-done.1 = f16[8,320,640]{2,1,0:T(8,128)(2,1)S(1)} async-done(((f16[8,320,640]{2,1,0:T(8,128)(2,1)}), f16[8,320,640]{2,1,0:T(8,128)(2,1)S(1)}, u32[]{:S(2)}, u32[]{:S(2)}) %all-to-all-start.1) | async-done | bytes 3276832 | tf_op jit(solution)/shard_map/all_to_all | solution.py:42
  138.3 0.7 fusion.19
  139.7 0.0 copy-start
  139.7 0.7 multiply_reduce_fusion
  140.4 0.8 copy-done
  141.3 2.9 %select_convert_fusion.1 = (f16[320,640]{1,0:T(8,128)(2,1)}, f32[320,640]{1,0:T(8,128)S(1)}) fusion(f32[]{:T(128)S(6)} %min.8, f32[]{:T(128)S(6)} %exp2.35, pred[640]{0:T(1024)(128)(4,1)S(1)} %iota_compare_fusion, f32[320,640]{1,0:T(8,128)S(1)} %multiply_reduce_fusion, bf16[576,1536]{0,1:T(8,128)(2,1)S(1)} %bitcast.20, bf16[2560,1536]{1,0:T(8,128)(2,1)} %bitcast.18, ...), kind=kOutput, calls=%fused_computation.11 | convolution fusion | flops 629964800 | bytes 4801164 | tf_op jit(solution)/shard_map/dot_general | solution.py:47
  144.2 14.9 %all-to-all-start.2 = ((f16[8,40,640]{2,1,0:T(8,128)(2,1)}), f16[8,40,640]{2,1,0:T(8,128)(2,1)S(1)}, u32[]{:S(2)}, u32[]{:S(2)}) async-start(f16[8,40,640]{2,1,0:T(8,128)(2,1)} %bitcast.9), calls=%async_computation.2 | async-start | bytes 819200 | tf_op jit(solution)/shard_map/all_to_all | solution.py:55
  159.1 18.3 %all-to-all-done.2 = f16[8,40,640]{2,1,0:T(8,128)(2,1)S(1)} async-done(((f16[8,40,640]{2,1,0:T(8,128)(2,1)}), f16[8,40,640]{2,1,0:T(8,128)(2,1)S(1)}, u32[]{:S(2)}, u32[]{:S(2)}) %all-to-all-start.2) | async-done | bytes 409632 | tf_op jit(solution)/shard_map/all_to_all | solution.py:55
  177.4 0.2 fusion.15
  177.6 0.1 multiply_reduce_fusion.1
  177.7 0.7 dynamic-slice_add_fusion
  (1 shorter events, 0.0 us)
Async XLA Ops:
  3.8 74.0 %all-to-all-start = ((bf16[12,576,128]{2,1,0:T(8,128)(2,1)}), bf16[12,576,128]{2,1,0:T(8,128)(2,1)S(1)}, u32[]{:S(2)}, u32[]{:S(2)}) async-start(bf16[12,576,128]{2,1,0:T(8,128)(2,1)} %bitcast.1), calls=%async_computation | async-start | bytes 3538944 | tf_op jit(solution)/shard_map/all_to_all | solution.py:28
  95.2 43.0 %all-to-all-start.1 = ((f16[8,320,640]{2,1,0:T(8,128)(2,1)}), f16[8,320,640]{2,1,0:T(8,128)(2,1)S(1)}, u32[]{:S(2)}, u32[]{:S(2)}) async-start(f16[8,320,640]{2,1,0:T(8,128)(2,1)} %bitcast.16), calls=%async_computation.1 | async-start | bytes 6553600 | tf_op jit(solution)/shard_map/all_to_all | solution.py:42
  139.7 1.5 copy-start
  144.2 33.2 %all-to-all-start.2 = ((f16[8,40,640]{2,1,0:T(8,128)(2,1)}), f16[8,40,640]{2,1,0:T(8,128)(2,1)S(1)}, u32[]{:S(2)}, u32[]{:S(2)}) async-start(f16[8,40,640]{2,1,0:T(8,128)(2,1)} %bitcast.9), calls=%async_computation.2 | async-start | bytes 819200 | tf_op jit(solution)/shard_map/all_to_all | solution.py:55

commit v2 on v1

--- a/solution.py
+++ b/solution.py
@@ -1,10 +1,13 @@
 import jax
 import jax.numpy as jnp
 from jax import lax
+from jax.experimental import pallas as pl
+from jax.experimental.pallas import tpu as pltpu
 from jax.sharding import Mesh, PartitionSpec as P
 
 SIZES = {"zh": 2, "yh": 4, "yl": 2, "x": 4, "chip": 6, "pair": 2}
 LIMIT = 60000.0
+ROWS = 512
 
 
 def decoded(code):
@@ -14,6 +17,41 @@
 def code_for(bound):
     e = jnp.floor(jnp.log2(LIMIT) - jnp.log2(jnp.maximum(bound, 1e-30)) - 0.01)
     return jnp.clip(e, -100.0, 100.0)
+
+
+def multiply(cot_ref, part_ref, out_ref, flat):
+    groups, w, t = part_ref.shape
+
+    @pl.when(pl.program_id(0) == 0)
+    def _():
+        for i in range(groups):
+            flat[:, i * t:(i + 1) * t] = part_ref[i]
+
+    out_ref[:, :w] = lax.dot_general(
+        cot_ref[...], flat[...], (((1,), (1,)), ((), ())), preferred_element_type=jnp.float32
+    )
+    out_ref[:, w:] = jnp.zeros((out_ref.shape[0], out_ref.shape[1] - w), jnp.float32)
+
+
+def product(cot, part, wide):
+    d, tokens = cot.shape
+    groups, w, t = part.shape
+    rows = min(ROWS, d)
+    return pl.pallas_call(
+        multiply,
+        grid=(d // rows,),
+        in_specs=[
+            pl.BlockSpec((rows, tokens), lambda i: (i, 0)),
+            pl.BlockSpec((groups, w, t), lambda i: (0, 0, 0)),
+        ],
+        out_specs=pl.BlockSpec((rows, wide), lambda i: (i, 0)),
+        out_shape=jax.ShapeDtypeStruct((d, wide), jnp.float32),
+        scratch_shapes=[pltpu.VMEM((w, tokens), jnp.bfloat16)],
+        compiler_params=pltpu.CompilerParams(vmem_limit_bytes=32 * 2**20),
+        cost_estimate=pl.CostEstimate(
+            flops=2 * d * tokens * w, bytes_accessed=2 * d * tokens + 4 * d * wide, transcendentals=0
+        ),
+    )(cot, part)
 
 
 def shards(hidden, cotangent):
@@ -32,19 +70,15 @@
     top = jnp.max(jnp.abs(cotangent)).astype(jnp.float32)
 
     code = code_for(top * jnp.max(jnp.abs(part)).astype(jnp.float32) * tokens)
-    part = part.transpose(1, 0, 2).reshape(w, tokens)
-    part = jnp.pad(part, ((0, wide - w), (0, 0)))
-    dims = (((1,), (1,)), ((), ()))
     lane = jnp.arange(wide) < w
 
-    terms = lax.dot_general(cot, part, dims, preferred_element_type=jnp.float32)
-    terms = jnp.where(lane, terms * decoded(code), code).astype(jnp.float16)
+    terms = product(cot, part, wide)
+    sent = jnp.where(lane, terms * decoded(code), code).astype(jnp.float16)
     got = lax.all_to_all(
-        terms.reshape(near, d // near, wide), ("yl", "x"), split_axis=0, concat_axis=0, tiled=True
+        sent.reshape(near, d // near, wide), ("yl", "x"), split_axis=0, concat_axis=0, tiled=True
     )
     me = lax.axis_index(("yl", "x"))
-    own = lax.dynamic_slice_in_dim(cot, me * (d // near), d // near, 0)
-    own = lax.dot_general(own, part, dims, preferred_element_type=jnp.float32)
+    own = lax.dynamic_slice_in_dim(terms, me * (d // near), d // near, 0)
     back = decoded(-got[:, 0, w].astype(jnp.float32))
     others = (jnp.arange(near) != me)
     weight = jnp.where(others, back, 0.0)[:, None, None]

time: 179 us -> 178 us (level)
  matrix products: 11.8 us -> 0 us
  Pallas kernels: 0 us -> 7.47 us
  other arithmetic: 8.17 us -> 12.9 us
    dot_general x2 -> x0, matrix products: 11.8 us -> none  [the longest x1 8.84 us: shards(): terms = lax.dot_general(cot, part, dims, preferred_element_type=jnp.float32)]
    pallas_call x0 -> x1, Pallas kernels: none -> 7.47 us  [product(): pl.pallas_call(multiply, grid=(d // rows,), in_specs=[pl.BlockSpec((rows,...]
    convert_element_type x0 -> x2, other arithmetic: none -> 4.68 us  [the longest x1 2.59 us: shards(): sent = jnp.where(lane, terms * decoded(code), code).astype(jnp.float16)]
    convert_element_type x1 -> x0, local copies, waits for them, and re-layouts: 3.97 us -> none  [shards(): terms = jnp.where(lane, terms * decoded(code), code).astype(jnp.float16)]
    unnamed x4 -> x5, local copies, waits for them, and re-layouts: 15.3 us -> 16.6 us
where the time goes in v2:
time: 178 us
  waiting for transfers between devices  94.9 us (53%)
  starting transfers between devices  32.8 us (18%)
  local copies, waits for them, and re-layouts  27.5 us (15%)
  other arithmetic  12.9 us (7%)
  Pallas kernels  7.47 us (4%)
  between operations  2.15 us (1%)
    all_to_all x1, waiting for transfers between devices, shards(): lax.all_to_all(hidden.T.reshape(groups, w, t), ('chip', 'pair'), split_ax...  39.3 us
    all_to_all x1, waiting for transfers between devices, shards(): lax.all_to_all(sent.reshape(near, d // near, wide), ('yl', 'x'), split_ax...  37.3 us
    all_to_all x1, waiting for transfers between devices, shards(): lax.all_to_all(sent.reshape(far, r, wide), ('zh', 'yh'), split_axis=0, co...  18.3 us
    unnamed x5, local copies, waits for them, and re-layouts  16.6 us
    all_to_all x1, starting transfers between devices, shards(): lax.all_to_all(sent.reshape(far, r, wide), ('zh', 'yh'), split_axis=0, co...  14.9 us
    all_to_all x1, starting transfers between devices, shards(): lax.all_to_all(hidden.T.reshape(groups, w, t), ('chip', 'pair'), split_ax...  12.1 us
    pallas_call x1, Pallas kernels, product(): pl.pallas_call(multiply, grid=(d // rows,), in_specs=[pl.BlockSpec((rows,...  7.47 us
    transpose x1, local copies, waits for them, and re-layouts, shards(): cotangent.reshape(tokens, far, near, r).transpose(2, 1, 3, 0)  7.1 us
  transfers between devices with their start and end apart: 3, of which 3 were waited for; matrix products, arithmetic and copies ran while one was open for 13% of the time, Pallas kernels for 0%

profile of v2, /device:TPU:10, one launch (start us, length us, event | category | flops | bytes accessed | tf_op | source)
XLA Modules:
  0.0 177.7 jit_solution(18693554037349883)
XLA Ops:
  0.0 3.8 %copy.17 = bf16[6912,128]{1,0:T(8,128)(2,1)} copy(bf16[6912,128]{0,1:T(8,128)(2,1)} %bitcast.11) | data formatting | bytes 3538944 | tf_op jit(solution)/shard_map/transpose | solution.py:67
  3.8 12.1 %all-to-all-start = ((bf16[12,576,128]{2,1,0:T(8,128)(2,1)}), bf16[12,576,128]{2,1,0:T(8,128)(2,1)S(1)}, u32[]{:S(2)}, u32[]{:S(2)}) async-start(bf16[12,576,128]{2,1,0:T(8,128)(2,1)} %bitcast.4), calls=%async_computation | async-start | bytes 3538944 | tf_op jit(solution)/shard_map/all_to_all | solution.py:66
  16.0 10.7 %copy.15 = bf16[1536,2560]{0,1:T(8,128)(2,1)} copy(bf16[1536,2560]{1,0:T(8,128)(2,1)} %param.3) | data formatting | bytes 15728640 | tf_op args[1]
  26.6 7.1 %copy.16 = bf16[8,8,40,1536]{3,2,1,0:T(8,128)(2,1)} copy(bf16[8,8,40,1536]{3,2,0,1:T(8,128)(2,1)} %bitcast.9) | data formatting | bytes 15728640 | tf_op jit(solution)/shard_map/transpose | solution.py:69
  33.7 4.8 %abs_reduce_fusion = bf16[]{:T(256)} fusion(bf16[1536,2560]{1,0:T(8,128)(2,1)} %param.3), kind=kLoop, calls=%fused_computation | loop fusion | flops 7864319 | bytes 7864322 | tf_op jit(solution)/shard_map/reduce_max | solution.py:70
  38.6 39.3 %all-to-all-done.part_ref = bf16[12,576,128]{2,1,0:T(8,128)(2,1)S(1)} async-done(((bf16[12,576,128]{2,1,0:T(8,128)(2,1)}), bf16[12,576,128]{2,1,0:T(8,128)(2,1)S(1)}, u32[]{:S(2)}, u32[]{:S(2)}) %all-to-all-start) | async-done | bytes 1769504 | tf_op jit(solution)/shard_map/all_to_all | solution.py:66
  77.9 0.9 abs_reduce_fusion.1
  80.1 0.0 copy-start.1
  80.1 3.2 %copy-done.1 = bf16[8,8,40,1536]{3,2,1,0:T(8,128)(2,1)S(1)} copy-done((bf16[8,8,40,1536]{3,2,1,0:T(8,128)(2,1)S(1)}, bf16[8,8,40,1536]{3,2,1,0:T(8,128)(2,1)}, u32[]{:S(2)}) %copy-start.1) | copy-done | bytes 7864344
  83.4 7.5 %shard_map.28 = f32[2560,640]{1,0:T(8,128)S(1)} custom-call(bf16[2560,1536]{1,0:T(8,128)(2,1)S(1)} %bitcast.8, bf16[12,576,128]{2,1,0:T(8,128)(2,1)S(1)} %all-to-all-done.part_ref), custom_call_target="tpu_custom_call" | custom-call | flops 4529848320 | bytes 14417920 | tf_op jit(solution)/shard_map/pallas_call | solution.py:40
  90.8 0.0 copy-start
  90.8 2.7 %copy-done = f32[2560,640]{1,0:T(8,128)} copy-done((f32[2560,640]{1,0:T(8,128)}, f32[2560,640]{1,0:T(8,128)S(1)}, u32[]{:S(2)}) %copy-start) | copy-done | bytes 6553624
  93.6 2.6 %select_convert_fusion = f16[2560,640]{1,0:T(8,128)(2,1)} fusion(f32[2560,640]{1,0:T(8,128)S(1)} %shard_map.28, f32[]{:T(128)S(6)} %min.7, f32[]{:T(128)S(6)} %exp2.31, pred[640]{0:T(1024)(128)(4,1)S(1)} %iota_compare_fusion), kind=kLoop, calls=%fused_computation.2 | loop fusion | flops 4915200 | bytes 9831048 | tf_op jit(solution)/shard_map/convert_element_type | solution.py:76
  96.2 5.7 %all-to-all-start.1 = ((f16[8,320,640]{2,1,0:T(8,128)(2,1)}), f16[8,320,640]{2,1,0:T(8,128)(2,1)S(1)}, u32[]{:S(2)}, u32[]{:S(2)}) async-start(f16[8,320,640]{2,1,0:T(8,128)(2,1)} %bitcast.10), calls=%async_computation.1 | async-start | bytes 6553600 | tf_op jit(solution)/shard_map/all_to_all | solution.py:77
  101.9 37.3 %all-to-all-done.1 = f16[8,320,640]{2,1,0:T(8,128)(2,1)S(1)} async-done(((f16[8,320,640]{2,1,0:T(8,128)(2,1)}), f16[8,320,640]{2,1,0:T(8,128)(2,1)S(1)}, u32[]{:S(2)}, u32[]{:S(2)}) %all-to-all-start.1) | async-done | bytes 3276832 | tf_op jit(solution)/shard_map/all_to_all | solution.py:77
  139.2 0.7 fusion.8
  140.6 0.7 multiply_reduce_fusion
  141.4 2.1 %select_convert_fusion.1 = (f16[320,640]{1,0:T(8,128)(2,1)}, f32[320,640]{1,0:T(8,128)S(1)}) fusion(f32[]{:T(128)S(6)} %min.8, f32[]{:T(128)S(6)} %exp2.35, pred[640]{0:T(1024)(128)(4,1)S(1)} %iota_compare_fusion, f32[320,640]{1,0:T(8,128)S(1)} %multiply_reduce_fusion, f32[2560,640]{1,0:T(8,128)} %copy-done, s32[]{:T(128)S(6)} %select_n.25), kind=kLoop, calls=%fused_computation.5 | loop fusion | flops 819200 | bytes 2867852 | tf_op jit(solution)/shard_map/convert_element_type | solution.py:88
  143.4 14.9 %all-to-all-start.2 = ((f16[8,40,640]{2,1,0:T(8,128)(2,1)}), f16[8,40,640]{2,1,0:T(8,128)(2,1)S(1)}, u32[]{:S(2)}, u32[]{:S(2)}) async-start(f16[8,40,640]{2,1,0:T(8,128)(2,1)} %bitcast.6), calls=%async_computation.2 | async-start | bytes 819200 | tf_op jit(solution)/shard_map/all_to_all | solution.py:89
  158.4 18.3 %all-to-all-done.2 = f16[8,40,640]{2,1,0:T(8,128)(2,1)S(1)} async-done(((f16[8,40,640]{2,1,0:T(8,128)(2,1)}), f16[8,40,640]{2,1,0:T(8,128)(2,1)S(1)}, u32[]{:S(2)}, u32[]{:S(2)}) %all-to-all-start.2) | async-done | bytes 409632 | tf_op jit(solution)/shard_map/all_to_all | solution.py:89
  176.7 0.2 fusion.7
  176.9 0.1 multiply_reduce_fusion.1
  177.0 0.7 dynamic-slice_add_fusion.1
  (1 shorter events, 0.0 us)
Async XLA Ops:
  3.8 74.0 %all-to-all-start = ((bf16[12,576,128]{2,1,0:T(8,128)(2,1)}), bf16[12,576,128]{2,1,0:T(8,128)(2,1)S(1)}, u32[]{:S(2)}, u32[]{:S(2)}) async-start(bf16[12,576,128]{2,1,0:T(8,128)(2,1)} %bitcast.4), calls=%async_computation | async-start | bytes 3538944 | tf_op jit(solution)/shard_map/all_to_all | solution.py:66
  80.1 3.2 %copy-start.1 = (bf16[8,8,40,1536]{3,2,1,0:T(8,128)(2,1)S(1)}, bf16[8,8,40,1536]{3,2,1,0:T(8,128)(2,1)}, u32[]{:S(2)}) copy-start(bf16[8,8,40,1536]{3,2,1,0:T(8,128)(2,1)} %copy.16) | copy-start | bytes 23592964
  90.8 2.7 %copy-start = (f32[2560,640]{1,0:T(8,128)}, f32[2560,640]{1,0:T(8,128)S(1)}, u32[]{:S(2)}) copy-start(f32[2560,640]{1,0:T(8,128)S(1)} %shard_map.28) | copy-start | bytes 19660804
  96.2 43.0 %all-to-all-start.1 = ((f16[8,320,640]{2,1,0:T(8,128)(2,1)}), f16[8,320,640]{2,1,0:T(8,128)(2,1)S(1)}, u32[]{:S(2)}, u32[]{:S(2)}) async-start(f16[8,320,640]{2,1,0:T(8,128)(2,1)} %bitcast.10), calls=%async_computation.1 | async-start | bytes 6553600 | tf_op jit(solution)/shard_map/all_to_all | solution.py:77
  143.4 33.2 %all-to-all-start.2 = ((f16[8,40,640]{2,1,0:T(8,128)(2,1)}), f16[8,40,640]{2,1,0:T(8,128)(2,1)S(1)}, u32[]{:S(2)}, u32[]{:S(2)}) async-start(f16[8,40,640]{2,1,0:T(8,128)(2,1)} %bitcast.6), calls=%async_computation.2 | async-start | bytes 819200 | tf_op jit(solution)/shard_map/all_to_all | solution.py:89

commit v3 on v2

--- a/solution.py
+++ b/solution.py
@@ -7,7 +7,6 @@
 
 SIZES = {"zh": 2, "yh": 4, "yl": 2, "x": 4, "chip": 6, "pair": 2}
 LIMIT = 60000.0
-ROWS = 512
 
 
 def decoded(code):
@@ -19,10 +18,11 @@
     return jnp.clip(e, -100.0, 100.0)
 
 
-def multiply(cot_ref, part_ref, out_ref, flat):
+def multiply(me_ref, cot_ref, part_ref, out_ref, own_ref, flat):
     groups, w, t = part_ref.shape
+    step, blocks = pl.program_id(0), out_ref.shape[0] // own_ref.shape[0]
 
-    @pl.when(pl.program_id(0) == 0)
+    @pl.when(step == 0)
     def _():
         for i in range(groups):
             flat[:, i * t:(i + 1) * t] = part_ref[i]
@@ -32,26 +32,40 @@
     )
     out_ref[:, w:] = jnp.zeros((out_ref.shape[0], out_ref.shape[1] - w), jnp.float32)
 
+    for i in range(blocks):
+        @pl.when(step * blocks + i == me_ref[0])
+        def _():
+            own_ref[...] = out_ref[i * own_ref.shape[0]:(i + 1) * own_ref.shape[0], :]
 
-def product(cot, part, wide):
+
+def product(cot, part, wide, me, near):
     d, tokens = cot.shape
     groups, w, t = part.shape
-    rows = min(ROWS, d)
+    rows = 2 * (d // near)
     return pl.pallas_call(
         multiply,
-        grid=(d // rows,),
-        in_specs=[
-            pl.BlockSpec((rows, tokens), lambda i: (i, 0)),
-            pl.BlockSpec((groups, w, t), lambda i: (0, 0, 0)),
+        grid_spec=pltpu.PrefetchScalarGridSpec(
+            num_scalar_prefetch=1,
+            grid=(d // rows,),
+            in_specs=[
+                pl.BlockSpec((rows, tokens), lambda i, _: (i, 0)),
+                pl.BlockSpec((groups, w, t), lambda i, _: (0, 0, 0)),
+            ],
+            out_specs=[
+                pl.BlockSpec((rows, wide), lambda i, _: (i, 0)),
+                pl.BlockSpec((d // near, wide), lambda i, _: (0, 0)),
+            ],
+            scratch_shapes=[pltpu.VMEM((w, tokens), jnp.bfloat16)],
+        ),
+        out_shape=[
+            jax.ShapeDtypeStruct((d, wide), jnp.float32),
+            jax.ShapeDtypeStruct((d // near, wide), jnp.float32),
         ],
-        out_specs=pl.BlockSpec((rows, wide), lambda i: (i, 0)),
-        out_shape=jax.ShapeDtypeStruct((d, wide), jnp.float32),
-        scratch_shapes=[pltpu.VMEM((w, tokens), jnp.bfloat16)],
-        compiler_params=pltpu.CompilerParams(vmem_limit_bytes=32 * 2**20),
+        compiler_params=pltpu.CompilerParams(vmem_limit_bytes=40 * 2**20),
         cost_estimate=pl.CostEstimate(
             flops=2 * d * tokens * w, bytes_accessed=2 * d * tokens + 4 * d * wide, transcendentals=0
         ),
-    )(cot, part)
+    )(me.astype(jnp.int32).reshape(1), cot, part)
 
 
 def shards(hidden, cotangent):
@@ -72,13 +86,12 @@
     code = code_for(top * jnp.max(jnp.abs(part)).astype(jnp.float32) * tokens)
     lane = jnp.arange(wide) < w
 
-    terms = product(cot, part, wide)
+    me = lax.axis_index(("yl", "x"))
+    terms, own = product(cot, part, wide, me, near)
     sent = jnp.where(lane, terms * decoded(code), code).astype(jnp.float16)
     got = lax.all_to_all(
         sent.reshape(near, d // near, wide), ("yl", "x"), split_axis=0, concat_axis=0, tiled=True
     )
-    me = lax.axis_index(("yl", "x"))
-    own = lax.dynamic_slice_in_dim(terms, me * (d // near), d // near, 0)
     back = decoded(-got[:, 0, w].astype(jnp.float32))
     others = (jnp.arange(near) != me)
     weight = jnp.where(others, back, 0.0)[:, None, None]

time: 178 us -> 174 us (0.978)
  the two profiles are of different devices: /device:TPU:10 before, /device:TPU:2 now
where the time goes in v3:
time: 174 us; the launch traced here: 173 us
  waiting for transfers between devices  56.5 us (32%)
  blocking collectives  43.6 us (25%)
  starting transfers between devices  27.1 us (16%)
  local copies, waits for them, and re-layouts  23.3 us (13%)
  other arithmetic  11.9 us (7%)
  Pallas kernels  8.88 us (5%)
  between operations  2.05 us (1%)
    all_to_all x1, blocking collectives, shards(): lax.all_to_all(sent.reshape(near, d // near, wide), ('yl', 'x'), split_ax...  43.6 us
    all_to_all x1, waiting for transfers between devices, shards(): lax.all_to_all(hidden.T.reshape(groups, w, t), ('chip', 'pair'), split_ax...  39.2 us
    all_to_all x1, waiting for transfers between devices, shards(): lax.all_to_all(sent.reshape(far, r, wide), ('zh', 'yh'), split_axis=0, co...  17.2 us
    all_to_all x1, starting transfers between devices, shards(): lax.all_to_all(sent.reshape(far, r, wide), ('zh', 'yh'), split_axis=0, co...  14.9 us
    unnamed x3, local copies, waits for them, and re-layouts  12.3 us
    all_to_all x1, starting transfers between devices, shards(): lax.all_to_all(hidden.T.reshape(groups, w, t), ('chip', 'pair'), split_ax...  12.1 us
    pallas_call x1, Pallas kernels, product(): pl.pallas_call(multiply, grid_spec=pltpu.PrefetchScalarGridSpec(num_scala...  8.88 us
    transpose x1, local copies, waits for them, and re-layouts, shards(): cotangent.reshape(tokens, far, near, r).transpose(2, 1, 3, 0)  7.1 us
  transfers between devices with their start and end apart: 2, of which 2 were waited for; matrix products, arithmetic and copies ran while one was open for 13% of the time, Pallas kernels for 0%

profile of v3, /device:TPU:2, one launch (start us, length us, event | category | flops | bytes accessed | tf_op | source)
XLA Modules:
  0.0 173.2 jit_solution(14441000795803358177)
XLA Ops:
  0.0 3.8 %copy.17 = bf16[6912,128]{1,0:T(8,128)(2,1)} copy(bf16[6912,128]{0,1:T(8,128)(2,1)} %bitcast.12) | data formatting | bytes 3538944 | tf_op jit(solution)/shard_map/transpose | solution.py:81
  3.8 12.1 %all-to-all-start = ((bf16[12,576,128]{2,1,0:T(8,128)(2,1)}), bf16[12,576,128]{2,1,0:T(8,128)(2,1)S(1)}, u32[]{:S(2)}, u32[]{:S(2)}) async-start(bf16[12,576,128]{2,1,0:T(8,128)(2,1)} %bitcast.5), calls=%async_computation | async-start | bytes 3538944 | tf_op jit(solution)/shard_map/all_to_all | solution.py:80
  16.0 10.7 %copy.15 = bf16[1536,2560]{0,1:T(8,128)(2,1)} copy(bf16[1536,2560]{1,0:T(8,128)(2,1)} %param.3) | data formatting | bytes 15728640 | tf_op args[1]
  26.6 7.1 %copy.16 = bf16[8,8,40,1536]{3,2,1,0:T(8,128)(2,1)} copy(bf16[8,8,40,1536]{3,2,0,1:T(8,128)(2,1)} %bitcast.9) | data formatting | bytes 15728640 | tf_op jit(solution)/shard_map/transpose | solution.py:83
  33.7 4.9 %abs_reduce_fusion = bf16[]{:T(256)} fusion(bf16[1536,2560]{1,0:T(8,128)(2,1)} %param.3), kind=kLoop, calls=%fused_computation | loop fusion | flops 7864319 | bytes 7864322 | tf_op jit(solution)/shard_map/reduce_max | solution.py:84
  38.6 39.2 %all-to-all-done.part_ref = bf16[12,576,128]{2,1,0:T(8,128)(2,1)S(1)} async-done(((bf16[12,576,128]{2,1,0:T(8,128)(2,1)}), bf16[12,576,128]{2,1,0:T(8,128)(2,1)S(1)}, u32[]{:S(2)}, u32[]{:S(2)}) %all-to-all-start) | async-done | bytes 1769504 | tf_op jit(solution)/shard_map/all_to_all | solution.py:80
  77.9 0.9 abs_reduce_fusion.1
  80.1 8.9 %shard_map.28 = (f32[2560,640]{1,0:T(8,128)S(1)}, f32[320,640]{1,0:T(8,128)S(1)}) custom-call(s32[1]{0:T(128)} %bitcast.me_ref, bf16[2560,1536]{1,0:T(8,128)(2,1)} %bitcast.11, bf16[12,576,128]{2,1,0:T(8,128)(2,1)S(1)} %all-to-all-done.part_ref), custom_call_target="tpu_custom_call" | custom-call | flops 4529848320 | bytes 14417920 | tf_op jit(solution)/shard_map/pallas_call | solution.py:45
  89.0 0.8 select_convert_fusion
  89.8 43.6 %all_to_all.15 = f16[8,320,640]{2,1,0:T(8,128)(2,1)S(1)} all-to-all(f16[8,320,640]{2,1,0:T(8,128)(2,1)S(1)} %bitcast.10), channel_id=1, replica_groups=mesh['zh'=2,'yh'=4,'yl'=2,'x'=4,'chip'=6,'pair'=2] {'yl','x'}, dimensions={0} | all-to-all | bytes 6553600 | tf_op jit(solution)/shard_map/all_to_all | solution.py:92
  133.3 0.0 copy-start
  133.3 1.7 copy-done
  135.0 0.7 fusion.8
  136.4 2.7 %multiply_reduce_fusion = f32[320,640]{1,0:T(8,128)S(1)} fusion(f16[8,320,640]{2,1,0:T(8,128)(2,1)} %copy-done, f32[8]{0:T(128)S(1)} %get-tuple-element.10), kind=kLoop, calls=%fused_computation.1 | loop fusion | flops 4710400 | bytes 4096032 | tf_op jit(solution)/shard_map/reduce_sum | solution.py:98
  139.1 0.9 select_convert_fusion.1
  140.0 14.9 %all-to-all-start.2 = ((f16[8,40,640]{2,1,0:T(8,128)(2,1)}), f16[8,40,640]{2,1,0:T(8,128)(2,1)S(1)}, u32[]{:S(2)}, u32[]{:S(2)}) async-start(f16[8,40,640]{2,1,0:T(8,128)(2,1)} %bitcast.7), calls=%async_computation.2 | async-start | bytes 819200 | tf_op jit(solution)/shard_map/all_to_all | solution.py:102
  154.9 17.2 %all-to-all-done.2 = f16[8,40,640]{2,1,0:T(8,128)(2,1)S(1)} async-done(((f16[8,40,640]{2,1,0:T(8,128)(2,1)}), f16[8,40,640]{2,1,0:T(8,128)(2,1)S(1)}, u32[]{:S(2)}, u32[]{:S(2)}) %all-to-all-start.2) | async-done | bytes 409632 | tf_op jit(solution)/shard_map/all_to_all | solution.py:102
  172.2 0.2 fusion.7
  172.4 0.1 multiply_reduce_fusion.1
  172.5 0.7 dynamic-slice_add_fusion
  (1 shorter events, 0.0 us)
Async XLA Ops:
  3.8 74.0 %all-to-all-start = ((bf16[12,576,128]{2,1,0:T(8,128)(2,1)}), bf16[12,576,128]{2,1,0:T(8,128)(2,1)S(1)}, u32[]{:S(2)}, u32[]{:S(2)}) async-start(bf16[12,576,128]{2,1,0:T(8,128)(2,1)} %bitcast.5), calls=%async_computation | async-start | bytes 3538944 | tf_op jit(solution)/shard_map/all_to_all | solution.py:80
  133.3 1.7 copy-start
  140.0 32.2 %all-to-all-start.2 = ((f16[8,40,640]{2,1,0:T(8,128)(2,1)}), f16[8,40,640]{2,1,0:T(8,128)(2,1)S(1)}, u32[]{:S(2)}, u32[]{:S(2)}) async-start(f16[8,40,640]{2,1,0:T(8,128)(2,1)} %bitcast.7), calls=%async_computation.2 | async-start | bytes 819200 | tf_op jit(solution)/shard_map/all_to_all | solution.py:102

commit v4 on v3

--- a/solution.py
+++ b/solution.py
@@ -25,10 +25,10 @@
     @pl.when(step == 0)
     def _():
         for i in range(groups):
-            flat[:, i * t:(i + 1) * t] = part_ref[i]
+            flat[i * t:(i + 1) * t, :] = part_ref[i].T
 
     out_ref[:, :w] = lax.dot_general(
-        cot_ref[...], flat[...], (((1,), (1,)), ((), ())), preferred_element_type=jnp.float32
+        cot_ref[...], flat[...], (((1,), (0,)), ((), ())), preferred_element_type=jnp.float32
     )
     out_ref[:, w:] = jnp.zeros((out_ref.shape[0], out_ref.shape[1] - w), jnp.float32)
 
@@ -55,7 +55,7 @@
                 pl.BlockSpec((rows, wide), lambda i, _: (i, 0)),
                 pl.BlockSpec((d // near, wide), lambda i, _: (0, 0)),
             ],
-            scratch_shapes=[pltpu.VMEM((w, tokens), jnp.bfloat16)],
+            scratch_shapes=[pltpu.VMEM((tokens, w), jnp.bfloat16)],
         ),
         out_shape=[
             jax.ShapeDtypeStruct((d, wide), jnp.float32),

time: 174 us -> 174 us (level)
  no operation moved by 1% of the time
where the time goes in v4:
time: 174 us; the launch traced here: 173 us
  waiting for transfers between devices  56.5 us (32%)
  blocking collectives  43.5 us (25%)
  starting transfers between devices  27.1 us (16%)
  local copies, waits for them, and re-layouts  23.3 us (13%)
  other arithmetic  11.9 us (7%)
  Pallas kernels  9.01 us (5%)
  between operations  2.05 us (1%)
    all_to_all x1, blocking collectives, shards(): lax.all_to_all(sent.reshape(near, d // near, wide), ('yl', 'x'), split_ax...  43.5 us
    all_to_all x1, waiting for transfers between devices, shards(): lax.all_to_all(hidden.T.reshape(groups, w, t), ('chip', 'pair'), split_ax...  39.2 us
    all_to_all x1, waiting for transfers between devices, shards(): lax.all_to_all(sent.reshape(far, r, wide), ('zh', 'yh'), split_axis=0, co...  17.2 us
    all_to_all x1, starting transfers between devices, shards(): lax.all_to_all(sent.reshape(far, r, wide), ('zh', 'yh'), split_axis=0, co...  14.9 us
    unnamed x3, local copies, waits for them, and re-layouts  12.3 us
    all_to_all x1, starting transfers between devices, shards(): lax.all_to_all(hidden.T.reshape(groups, w, t), ('chip', 'pair'), split_ax...  12.1 us
    pallas_call x1, Pallas kernels, product(): pl.pallas_call(multiply, grid_spec=pltpu.PrefetchScalarGridSpec(num_scala...  9.01 us
    transpose x1, local copies, waits for them, and re-layouts, shards(): cotangent.reshape(tokens, far, near, r).transpose(2, 1, 3, 0)  7.1 us
  transfers between devices with their start and end apart: 2, of which 2 were waited for; matrix products, arithmetic and copies ran while one was open for 13% of the time, Pallas kernels for 0%

profile of v4, /device:TPU:2, one launch (start us, length us, event | category | flops | bytes accessed | tf_op | source)
XLA Modules:
  0.0 173.3 jit_solution(7907773331429341513)
XLA Ops:
  0.0 3.8 %copy.17 = bf16[6912,128]{1,0:T(8,128)(2,1)} copy(bf16[6912,128]{0,1:T(8,128)(2,1)} %bitcast.12) | data formatting | bytes 3538944 | tf_op jit(solution)/shard_map/transpose | solution.py:81
  3.8 12.1 %all-to-all-start = ((bf16[12,576,128]{2,1,0:T(8,128)(2,1)}), bf16[12,576,128]{2,1,0:T(8,128)(2,1)S(1)}, u32[]{:S(2)}, u32[]{:S(2)}) async-start(bf16[12,576,128]{2,1,0:T(8,128)(2,1)} %bitcast.5), calls=%async_computation | async-start | bytes 3538944 | tf_op jit(solution)/shard_map/all_to_all | solution.py:80
  16.0 10.7 %copy.15 = bf16[1536,2560]{0,1:T(8,128)(2,1)} copy(bf16[1536,2560]{1,0:T(8,128)(2,1)} %param.3) | data formatting | bytes 15728640 | tf_op args[1]
  26.6 7.1 %copy.16 = bf16[8,8,40,1536]{3,2,1,0:T(8,128)(2,1)} copy(bf16[8,8,40,1536]{3,2,0,1:T(8,128)(2,1)} %bitcast.9) | data formatting | bytes 15728640 | tf_op jit(solution)/shard_map/transpose | solution.py:83
  33.7 4.9 %abs_reduce_fusion = bf16[]{:T(256)} fusion(bf16[1536,2560]{1,0:T(8,128)(2,1)} %param.3), kind=kLoop, calls=%fused_computation | loop fusion | flops 7864319 | bytes 7864322 | tf_op jit(solution)/shard_map/reduce_max | solution.py:84
  38.6 39.2 %all-to-all-done.part_ref = bf16[12,576,128]{2,1,0:T(8,128)(2,1)S(1)} async-done(((bf16[12,576,128]{2,1,0:T(8,128)(2,1)}), bf16[12,576,128]{2,1,0:T(8,128)(2,1)S(1)}, u32[]{:S(2)}, u32[]{:S(2)}) %all-to-all-start) | async-done | bytes 1769504 | tf_op jit(solution)/shard_map/all_to_all | solution.py:80
  77.9 0.9 abs_reduce_fusion.1
  80.1 9.0 %shard_map.28 = (f32[2560,640]{1,0:T(8,128)S(1)}, f32[320,640]{1,0:T(8,128)S(1)}) custom-call(s32[1]{0:T(128)} %bitcast.me_ref, bf16[2560,1536]{1,0:T(8,128)(2,1)} %bitcast.11, bf16[12,576,128]{2,1,0:T(8,128)(2,1)S(1)} %all-to-all-done.part_ref), custom_call_target="tpu_custom_call" | custom-call | flops 4529848320 | bytes 14417920 | tf_op jit(solution)/shard_map/pallas_call | solution.py:45
  89.1 0.8 select_convert_fusion
  89.9 43.5 %all_to_all.15 = f16[8,320,640]{2,1,0:T(8,128)(2,1)S(1)} all-to-all(f16[8,320,640]{2,1,0:T(8,128)(2,1)S(1)} %bitcast.10), channel_id=1, replica_groups=mesh['zh'=2,'yh'=4,'yl'=2,'x'=4,'chip'=6,'pair'=2] {'yl','x'}, dimensions={0} | all-to-all | bytes 6553600 | tf_op jit(solution)/shard_map/all_to_all | solution.py:92
  133.5 0.0 copy-start
  133.5 1.7 copy-done
  135.2 0.7 fusion.8
  136.5 2.7 %multiply_reduce_fusion = f32[320,640]{1,0:T(8,128)S(1)} fusion(f16[8,320,640]{2,1,0:T(8,128)(2,1)} %copy-done, f32[8]{0:T(128)S(1)} %get-tuple-element.10), kind=kLoop, calls=%fused_computation.1 | loop fusion | flops 4710400 | bytes 4096032 | tf_op jit(solution)/shard_map/reduce_sum | solution.py:98
  139.2 0.9 select_convert_fusion.1
  140.1 14.9 %all-to-all-start.2 = ((f16[8,40,640]{2,1,0:T(8,128)(2,1)}), f16[8,40,640]{2,1,0:T(8,128)(2,1)S(1)}, u32[]{:S(2)}, u32[]{:S(2)}) async-start(f16[8,40,640]{2,1,0:T(8,128)(2,1)} %bitcast.7), calls=%async_computation.2 | async-start | bytes 819200 | tf_op jit(solution)/shard_map/all_to_all | solution.py:102
  155.1 17.2 %all-to-all-done.2 = f16[8,40,640]{2,1,0:T(8,128)(2,1)S(1)} async-done(((f16[8,40,640]{2,1,0:T(8,128)(2,1)}), f16[8,40,640]{2,1,0:T(8,128)(2,1)S(1)}, u32[]{:S(2)}, u32[]{:S(2)}) %all-to-all-start.2) | async-done | bytes 409632 | tf_op jit(solution)/shard_map/all_to_all | solution.py:102
  172.3 0.2 fusion.7
  172.5 0.1 multiply_reduce_fusion.1
  172.7 0.7 dynamic-slice_add_fusion
  (1 shorter events, 0.0 us)
Async XLA Ops:
  3.8 74.0 %all-to-all-start = ((bf16[12,576,128]{2,1,0:T(8,128)(2,1)}), bf16[12,576,128]{2,1,0:T(8,128)(2,1)S(1)}, u32[]{:S(2)}, u32[]{:S(2)}) async-start(bf16[12,576,128]{2,1,0:T(8,128)(2,1)} %bitcast.5), calls=%async_computation | async-start | bytes 3538944 | tf_op jit(solution)/shard_map/all_to_all | solution.py:80
  133.5 1.7 copy-start
  140.1 32.2 %all-to-all-start.2 = ((f16[8,40,640]{2,1,0:T(8,128)(2,1)}), f16[8,40,640]{2,1,0:T(8,128)(2,1)S(1)}, u32[]{:S(2)}, u32[]{:S(2)}) async-start(f16[8,40,640]{2,1,0:T(8,128)(2,1)} %bitcast.7), calls=%async_computation.2 | async-start | bytes 819200 | tf_op jit(solution)/shard_map/all_to_all | solution.py:102

commit v5 on v3

--- a/solution.py
+++ b/solution.py
@@ -16,6 +16,23 @@
 def code_for(bound):
     e = jnp.floor(jnp.log2(LIMIT) - jnp.log2(jnp.maximum(bound, 1e-30)) - 0.01)
     return jnp.clip(e, -100.0, 100.0)
+
+
+def turn(in_ref, out_ref):
+    out_ref[...] = in_ref[...].T
+
+
+def turned(hidden):
+    t, ff = hidden.shape
+    piece = ff // 3
+    return pl.pallas_call(
+        turn,
+        grid=(3,),
+        in_specs=[pl.BlockSpec((t, piece), lambda i: (0, i))],
+        out_specs=pl.BlockSpec((piece, t), lambda i: (i, 0)),
+        out_shape=jax.ShapeDtypeStruct((ff, t), hidden.dtype),
+        compiler_params=pltpu.CompilerParams(vmem_limit_bytes=40 * 2**20),
+    )(hidden)
 
 
 def multiply(me_ref, cot_ref, part_ref, out_ref, own_ref, flat):
@@ -78,7 +95,7 @@
     r = d // (near * far)
 
     part = lax.all_to_all(
-        hidden.T.reshape(groups, w, t), ("chip", "pair"), split_axis=0, concat_axis=0, tiled=True
+        turned(hidden).reshape(groups, w, t), ("chip", "pair"), split_axis=0, concat_axis=0, tiled=True
     )
     cot = cotangent.reshape(tokens, far, near, r).transpose(2, 1, 3, 0).reshape(d, tokens)
     top = jnp.max(jnp.abs(cotangent)).astype(jnp.float32)

time: 174 us -> 174 us (level)
  local copies, waits for them, and re-layouts: 23.3 us -> 20.9 us
  Pallas kernels: 8.88 us -> 11 us
    transpose x1 -> x0, local copies, waits for them, and re-layouts: 3.83 us -> none  [shards(): hidden.T.reshape(groups, w, t)]
    pallas_call x0 -> x1, Pallas kernels: none -> 2.14 us  [turned(): pl.pallas_call(turn, grid=(3,), in_specs=[pl.BlockSpec((t, piece), lambda...]
    unnamed x3 -> x5, local copies, waits for them, and re-layouts: 12.3 us -> 13.8 us
where the time goes in v5:
time: 174 us; the launch traced here: 173 us
  waiting for transfers between devices  56.5 us (32%)
  blocking collectives  43.6 us (25%)
  starting transfers between devices  27.1 us (16%)
  local copies, waits for them, and re-layouts  20.9 us (12%)
  other arithmetic  11.9 us (7%)
  Pallas kernels  11 us (6%)
  between operations  2.05 us (1%)
    all_to_all x1, blocking collectives, shards(): lax.all_to_all(sent.reshape(near, d // near, wide), ('yl', 'x'), split_ax...  43.6 us
    all_to_all x1, waiting for transfers between devices, shards(): lax.all_to_all(turned(hidden).reshape(groups, w, t), ('chip', 'pair'), sp...  39.2 us
    all_to_all x1, waiting for transfers between devices, shards(): lax.all_to_all(sent.reshape(far, r, wide), ('zh', 'yh'), split_axis=0, co...  17.2 us
    all_to_all x1, starting transfers between devices, shards(): lax.all_to_all(sent.reshape(far, r, wide), ('zh', 'yh'), split_axis=0, co...  14.9 us
    unnamed x5, local copies, waits for them, and re-layouts  13.8 us
    all_to_all x1, starting transfers between devices, shards(): lax.all_to_all(turned(hidden).reshape(groups, w, t), ('chip', 'pair'), sp...  12.1 us
    pallas_call x1, Pallas kernels, product(): pl.pallas_call(multiply, grid_spec=pltpu.PrefetchScalarGridSpec(num_scala...  8.87 us
    transpose x1, local copies, waits for them, and re-layouts, shards(): cotangent.reshape(tokens, far, near, r).transpose(2, 1, 3, 0)  7.1 us
  transfers between devices with their start and end apart: 2, of which 2 were waited for; matrix products, arithmetic and copies ran while one was open for 13% of the time, Pallas kernels for 0%

profile of v5, /device:TPU:2, one launch (start us, length us, event | category | flops | bytes accessed | tf_op | source)
XLA Modules:
  0.0 173.0 jit_solution(3462124307930829262)
XLA Ops:
  0.0 0.0 copy-start
  0.0 1.5 copy-done
  1.5 2.1 %shard_map.28 = bf16[6912,128]{1,0:T(8,128)(2,1)} custom-call(bf16[128,6912]{1,0:T(8,128)(2,1)S(1)} %copy-done), custom_call_target="tpu_custom_call" | custom-call | tf_op jit(solution)/shard_map/pallas_call | solution.py:28
  3.6 12.1 %all-to-all-start = ((bf16[12,576,128]{2,1,0:T(8,128)(2,1)}), bf16[12,576,128]{2,1,0:T(8,128)(2,1)S(1)}, u32[]{:S(2)}, u32[]{:S(2)}) async-start(bf16[12,576,128]{2,1,0:T(8,128)(2,1)} %bitcast.4), calls=%async_computation | async-start | bytes 3538944 | tf_op jit(solution)/shard_map/all_to_all | solution.py:97
  15.8 10.7 %copy.12 = bf16[1536,2560]{0,1:T(8,128)(2,1)} copy(bf16[1536,2560]{1,0:T(8,128)(2,1)} %param.3) | data formatting | bytes 15728640 | tf_op args[1]
  26.4 7.1 %copy.13 = bf16[8,8,40,1536]{3,2,1,0:T(8,128)(2,1)} copy(bf16[8,8,40,1536]{3,2,0,1:T(8,128)(2,1)} %bitcast.8) | data formatting | bytes 15728640 | tf_op jit(solution)/shard_map/transpose | solution.py:100
  33.5 4.9 %abs_reduce_fusion = bf16[]{:T(256)} fusion(bf16[1536,2560]{1,0:T(8,128)(2,1)} %param.3), kind=kLoop, calls=%fused_computation | loop fusion | flops 7864319 | bytes 7864322 | tf_op jit(solution)/shard_map/reduce_max | solution.py:101
  38.4 39.2 %all-to-all-done.part_ref = bf16[12,576,128]{2,1,0:T(8,128)(2,1)S(1)} async-done(((bf16[12,576,128]{2,1,0:T(8,128)(2,1)}), bf16[12,576,128]{2,1,0:T(8,128)(2,1)S(1)}, u32[]{:S(2)}, u32[]{:S(2)}) %all-to-all-start) | async-done | bytes 1769504 | tf_op jit(solution)/shard_map/all_to_all | solution.py:97
  77.7 0.9 abs_reduce_fusion.1
  79.9 8.9 %shard_map.29 = (f32[2560,640]{1,0:T(8,128)S(1)}, f32[320,640]{1,0:T(8,128)S(1)}) custom-call(s32[1]{0:T(128)} %bitcast.me_ref, bf16[2560,1536]{1,0:T(8,128)(2,1)} %bitcast.10, bf16[12,576,128]{2,1,0:T(8,128)(2,1)S(1)} %all-to-all-done.part_ref), custom_call_target="tpu_custom_call" | custom-call | flops 4529848320 | bytes 14417920 | tf_op jit(solution)/shard_map/pallas_call | solution.py:62
  88.8 0.8 select_convert_fusion
  89.6 43.6 %all_to_all.15 = f16[8,320,640]{2,1,0:T(8,128)(2,1)S(1)} all-to-all(f16[8,320,640]{2,1,0:T(8,128)(2,1)S(1)} %bitcast.9), channel_id=1, replica_groups=mesh['zh'=2,'yh'=4,'yl'=2,'x'=4,'chip'=6,'pair'=2] {'yl','x'}, dimensions={0} | all-to-all | bytes 6553600 | tf_op jit(solution)/shard_map/all_to_all | solution.py:109
  133.1 0.0 copy-start.1
  133.1 1.7 copy-done.1
  134.8 0.7 fusion.8
  136.2 2.7 %multiply_reduce_fusion = f32[320,640]{1,0:T(8,128)S(1)} fusion(f16[8,320,640]{2,1,0:T(8,128)(2,1)} %copy-done.1, f32[8]{0:T(128)S(1)} %get-tuple-element.10), kind=kLoop, calls=%fused_computation.1 | loop fusion | flops 4710400 | bytes 4096032 | tf_op jit(solution)/shard_map/reduce_sum | solution.py:115
  138.9 0.9 select_convert_fusion.1
  139.8 14.9 %all-to-all-start.2 = ((f16[8,40,640]{2,1,0:T(8,128)(2,1)}), f16[8,40,640]{2,1,0:T(8,128)(2,1)S(1)}, u32[]{:S(2)}, u32[]{:S(2)}) async-start(f16[8,40,640]{2,1,0:T(8,128)(2,1)} %bitcast.6), calls=%async_computation.2 | async-start | bytes 819200 | tf_op jit(solution)/shard_map/all_to_all | solution.py:119
  154.7 17.2 %all-to-all-done.2 = f16[8,40,640]{2,1,0:T(8,128)(2,1)S(1)} async-done(((f16[8,40,640]{2,1,0:T(8,128)(2,1)}), f16[8,40,640]{2,1,0:T(8,128)(2,1)S(1)}, u32[]{:S(2)}, u32[]{:S(2)}) %all-to-all-start.2) | async-done | bytes 409632 | tf_op jit(solution)/shard_map/all_to_all | solution.py:119
  172.0 0.2 fusion.7
  172.2 0.1 multiply_reduce_fusion.1
  172.3 0.7 dynamic-slice_add_fusion
  (1 shorter events, 0.0 us)
Async XLA Ops:
  0.0 1.5 copy-start
  3.6 74.0 %all-to-all-start = ((bf16[12,576,128]{2,1,0:T(8,128)(2,1)}), bf16[12,576,128]{2,1,0:T(8,128)(2,1)S(1)}, u32[]{:S(2)}, u32[]{:S(2)}) async-start(bf16[12,576,128]{2,1,0:T(8,128)(2,1)} %bitcast.4), calls=%async_computation | async-start | bytes 3538944 | tf_op jit(solution)/shard_map/all_to_all | solution.py:97
  133.1 1.7 copy-start.1
  139.8 32.2 %all-to-all-start.2 = ((f16[8,40,640]{2,1,0:T(8,128)(2,1)}), f16[8,40,640]{2,1,0:T(8,128)(2,1)S(1)}, u32[]{:S(2)}, u32[]{:S(2)}) async-start(f16[8,40,640]{2,1,0:T(8,128)(2,1)} %bitcast.6), calls=%async_computation.2 | async-start | bytes 819200 | tf_op jit(solution)/shard_map/all_to_all | solution.py:119
